TPU v7x, 32 devices: a whole 2x2x4 slice. The times are simulated.
32 devices in a mesh: ctx: 8 (over z, y), tp: 4 (over x, core).
Axes of the slice: x: 2, y: 2, z: 4, core: 2. Of those that a mesh axis runs over, the one named last changes fastest.
Arguments:
- features: bfloat16 [3, 2048, 1024], P(None, 'tp', 'ctx'), may hold values from -6 to 6
- short_taps: float32 [3, 3, 2048], P(None, None, 'tp'), may hold values from -3 to 3
- filters: bfloat16 [128, 1024], P('tp'), may hold values from -2 to 2
- skip_gain: float32 [2048], P('tp'), may hold values from -4 to 4
- out_weight: bfloat16 [2048, 2048], P('tp'), may hold values from -0.125 to 0.125
Outputs:
- block_out: bfloat16 [2048, 1024], P('tp', 'ctx')
All inputs are finite; a program needn't handle non-finite values.
Results may differ from a plain program's by a relative error of at most 0.009.
Values may be sent and summed in bfloat16 or wider, within the bound.
A program may use at most 64 MiB of HBM per device.

v0:
```python
import math

import jax
import jax.numpy as jnp
from jax import lax
from jax.sharding import PartitionSpec as P

GROUP = 16


highest = lax.Precision.HIGHEST


def from_behind(value, axis, steps):
    count = lax.axis_size(axis)
    initial, last = (max(0, -steps), min(count, count - steps))
    return lax.ppermute(value, axis, [(source, source + steps) for source in range(initial, last)])


def left_product(matrix, stacked):
    return jnp.einsum("kn,bns->bks", matrix, stacked, precision=highest)


def right_product(stacked, matrix):
    return jnp.einsum("bks,st->bkt", stacked, matrix, precision=highest)


def split_length(total_len):
    row_count = 2
    for candidate in range(2, math.isqrt(total_len) + 1, 2):
        if total_len % candidate == 0:
            row_count = candidate
    return (row_count, total_len // row_count)


def dft_tables(row_count, col_count):
    total_len = row_count * col_count
    row_index = jnp.arange(row_count, dtype=jnp.int32)
    col_index = jnp.arange(col_count, dtype=jnp.int32)
    row_angle = (row_index[:, None] * row_index[None, :] % row_count).astype(jnp.float32) * (
        2.0 * math.pi / row_count
    )
    col_angle = (col_index[:, None] * col_index[None, :] % col_count).astype(jnp.float32) * (
        2.0 * math.pi / col_count
    )
    twist_angle = (row_index[:, None] * col_index[None, :] % total_len).astype(jnp.float32) * (
        2.0 * math.pi / total_len
    )
    return (
        jnp.cos(row_angle),
        jnp.sin(row_angle),
        jnp.cos(col_angle),
        jnp.sin(col_angle),
        jnp.cos(twist_angle),
        jnp.sin(twist_angle),
    )


def forward_dft(signal, tables):
    cos_row, sin_row, cos_col, sin_col, cos_twist, sin_twist = tables
    half_rows = signal.shape[1]
    first_real = left_product(cos_row[:, :half_rows], signal)
    first_imag = -left_product(sin_row[:, :half_rows], signal)
    twist_real = first_real * cos_twist + first_imag * sin_twist
    twist_imag = first_imag * cos_twist - first_real * sin_twist
    spec_real = right_product(twist_real, cos_col) + right_product(twist_imag, sin_col)
    spec_imag = right_product(twist_imag, cos_col) - right_product(twist_real, sin_col)
    return (spec_real, spec_imag)


def inverse_dft(spec_real, spec_imag, tables, half_rows):
    cos_row, sin_row, cos_col, sin_col, cos_twist, sin_twist = tables
    total_len = cos_row.shape[0] * cos_col.shape[0]
    middle_real = right_product(spec_real, cos_col) - right_product(spec_imag, sin_col)
    middle_imag = right_product(spec_imag, cos_col) + right_product(spec_real, sin_col)
    turned_real = middle_real * cos_twist - middle_imag * sin_twist
    turned_imag = middle_imag * cos_twist + middle_real * sin_twist
    signal = left_product(cos_row[:half_rows, :], turned_real) - left_product(
        sin_row[:half_rows, :], turned_imag
    )
    return signal / total_len


def local(features, short_taps, filters, skip_gain, out_weight):
    taps_count = short_taps.shape[0]
    chan_tp = features.shape[1]
    tok_local = features.shape[2]
    ctx_count = lax.axis_size("ctx")
    chan_dev = chan_tp // ctx_count
    group_dev = max(1, chan_dev // GROUP)
    per_group = chan_dev // group_dev
    seq_len = tok_local * ctx_count
    row_count, col_count = split_length(2 * seq_len)
    half_rows = row_count // 2
    tables = dft_tables(row_count, col_count)
    ctx_rank = lax.axis_index("ctx")
    kernel_rows = lax.dynamic_slice_in_dim(filters, ctx_rank * chan_dev // GROUP, group_dev, 0)
    kernel_real, kernel_imag = forward_dft(
        kernel_rows.astype(jnp.float32).reshape(group_dev, half_rows, col_count), tables
    )
    previous = from_behind(features[:, :, tok_local - (taps_count - 1) :], "ctx", 1)
    extended = jnp.concatenate([previous, features], axis=2).astype(jnp.float32)
    conv_all = jnp.zeros(features.shape, jnp.float32)
    for offset in range(taps_count):
        begin_at = taps_count - 1 - offset
        conv_all = (
            conv_all
            + short_taps[offset][:, :, None] * extended[:, :, begin_at : begin_at + tok_local]
        )
    query_conv = conv_all[0]
    product = (conv_all[1] * conv_all[2]).astype(jnp.bfloat16)
    gathered = lax.all_to_all(product, "ctx", split_axis=0, concat_axis=1, tiled=True)
    signal = gathered.astype(jnp.float32)
    sig_real, sig_imag = forward_dft(signal.reshape(chan_dev, half_rows, col_count), tables)
    four_shape = (group_dev, per_group, row_count, col_count)
    sig_real = sig_real.reshape(four_shape)
    sig_imag = sig_imag.reshape(four_shape)
    kernel_wide_real = kernel_real[:, None]
    kernel_wide_imag = kernel_imag[:, None]
    prod_real = (sig_real * kernel_wide_real - sig_imag * kernel_wide_imag).reshape(
        chan_dev, row_count, col_count
    )
    prod_imag = (sig_real * kernel_wide_imag + sig_imag * kernel_wide_real).reshape(
        chan_dev, row_count, col_count
    )
    longconv = inverse_dft(prod_real, prod_imag, tables, half_rows).reshape(chan_dev, seq_len)
    skip_local = lax.dynamic_slice_in_dim(skip_gain, ctx_rank * chan_dev, chan_dev, 0)
    long_mix = (longconv + skip_local[:, None] * signal).astype(jnp.bfloat16)
    restored = lax.all_to_all(long_mix, "ctx", split_axis=1, concat_axis=0, tiled=True)
    gated = (query_conv * restored.astype(jnp.float32)).astype(jnp.bfloat16)
    return lax.psum_scatter(
        lax.dot_general(
            out_weight, gated, (((0,), (0,)), ((), ())), preferred_element_type=jnp.float32
        ).astype(jnp.bfloat16),
        "tp",
        scatter_dimension=0,
        tiled=True,
    )


def solution(mesh):
    placed = (P(None, "tp", "ctx"), P(None, None, "tp"), P("tp", None), P("tp"), P("tp", None))
    return jax.shard_map(
        local, mesh=mesh, in_specs=placed, out_specs=P("tp", "ctx"), check_vma=False
    )
```

profile of v0, /device:TPU:0, one launch (start us, length us, event | category | flops | bytes accessed | tf_op | source)
XLA Modules:
  0.0 98.0 jit_solution(16788445554689319216)
XLA Ops:
  6.5 2.1 %slice.49 = bf16[3,512,2]{2,1,0:T(8,128)(2,1)} slice(bf16[3,512,128]{2,1,0:T(8,128)(2,1)} %param.5), slice={[0:3], [0:512], [126:128]} | slice | bytes 12288 | tf_op jit(solution)/shard_map/slice | solution.py:101
  8.6 4.9 %collective-permute-start = (bf16[3,512,2]{2,1,0:T(8,128)(2,1)}, bf16[3,512,2]{2,1,0:T(8,128)(2,1)S(1)}, u32[]{:S(2)}, u32[]{:S(2)}) collective-permute-start(bf16[3,512,2]{2,1,0:T(8,128)(2,1)} %slice.49), channel_id=1, source_target_pairs={{0,4},{4,8},{8,12},{12,16},{16,20},{20,24},{24,28},{1,5},{5,9},{9,... | collective-permute-start | bytes 18440 | tf_op jit(solution)/shard_map/ppermute | solution.py:17
  13.8 0.8 constant_dynamic-slice_fusion
  15.1 0.3 fusion.47
  15.5 0.3 fusion.50
  15.8 0.3 convolution_subtract_fusion.3
  16.2 5.9 %collective-permute-done = bf16[3,512,2]{2,1,0:T(8,128)(2,1)S(1)} collective-permute-done((bf16[3,512,2]{2,1,0:T(8,128)(2,1)}, bf16[3,512,2]{2,1,0:T(8,128)(2,1)S(1)}, u32[]{:S(2)}, u32[]{:S(2)}) %collective-permute-start) | collective-permute-done | bytes 6176 | tf_op jit(solution)/shard_map/ppermute | solution.py:17
  22.5 1.2 %fusion.26 = f32[3,512,128]{2,1,0:T(8,128)S(1)} fusion(f32[3,512,130]{2,1,0:T(8,128)S(1)} %maximum_convert_fusion, f32[3,512]{1,0:T(4,128)S(1)} %get-tuple-element.10, f32[3,512]{1,0:T(4,128)S(1)} %get-tuple-element.11, f32[3,512]{1,0:T(4,128)S(1)} %get-tuple-element.9), kind=kLoop, calls=%fused_computation.45 | loop fusion | flops 983040 | bytes 3164160 | tf_op jit(solution)/shard_map/add | solution.py:107
  23.7 0.7 fusion.32
  24.4 6.7 %all-to-all-start = ((bf16[8,64,128]{2,1,0:T(8,128)(2,1)}), bf16[8,64,128]{2,1,0:T(8,128)(2,1)S(1)}, u32[]{:S(2)}, u32[]{:S(2)}) async-start(bf16[8,64,128]{2,1,0:T(8,128)(2,1)} %bitcast.4), calls=%async_computation | async-start | bytes 262144 | tf_op jit(solution)/shard_map/all_to_all | solution.py:112
  31.3 0.3 convolution_add_fusion.2
  31.6 0.7 copy.24
  32.3 1.3 %dynamic_slice.7 = f32[64]{0:T(128)} dynamic-slice(f32[512]{0:T(512)} %param.8, s32[]{:T(128)S(6)} %select_n.95), dynamic_slice_sizes={64} | dynamic-slice | bytes 516 | tf_op jit(solution)/shard_map/dynamic_slice | solution.py:127
  33.6 4.8 %all-to-all-done = bf16[8,64,128]{2,1,0:T(8,128)(2,1)S(1)} async-done(((bf16[8,64,128]{2,1,0:T(8,128)(2,1)}), bf16[8,64,128]{2,1,0:T(8,128)(2,1)S(1)}, u32[]{:S(2)}, u32[]{:S(2)}) %all-to-all-start) | async-done | bytes 131104 | tf_op jit(solution)/shard_map/all_to_all | solution.py:112
  38.6 0.6 convolution_bitcast_fusion
  39.3 0.8 multiply_add_fusion
  40.1 1.8 %fusion.24 = f32[64,32,64]{2,0,1:T(8,128)S(1)} fusion(f32[64,32,64]{2,1,0:T(8,128)S(1)} %get-tuple-element.7), kind=kOutput, calls=%fused_computation.42 | convolution fusion | flops 100720640 | bytes 1048576 | tf_op jit(solution)/shard_map/bks,st->bkt/dot_general | solution.py:25
  41.9 1.8 %fusion.20 = f32[64,32,64]{2,0,1:T(8,128)S(1)} fusion(f32[64,32,64]{2,1,0:T(8,128)S(1)} %get-tuple-element.8), kind=kOutput, calls=%fused_computation.38 | convolution fusion | flops 100720640 | bytes 1048576 | tf_op jit(solution)/shard_map/bks,st->bkt/dot_general | solution.py:25
  43.7 1.8 %convolution_subtract_fusion.1 = f32[64,32,64]{2,0,1:T(8,128)S(1)} fusion(f32[64,32,64]{2,0,1:T(8,128)S(1)} %fusion.20, f32[64,32,64]{2,1,0:T(8,128)S(1)} %get-tuple-element.7), kind=kOutput, calls=%fused_computation.8 | convolution fusion | flops 100851712 | bytes 1572864 | tf_op jit(solution)/shard_map/bks,st->bkt/dot_general | solution.py:25
  45.5 2.0 %fusion.5 = (f32[64,32,64]{2,0,1:T(8,128)S(1)}, f32[64,32,64]{2,0,1:T(8,128)S(1)}) fusion(f32[64,32,64]{2,0,1:T(8,128)S(1)} %convolution_subtract_fusion.1, f32[4,32,64]{2,0,1:T(4,128)S(1)} %copy.27, f32[4,32,64]{2,0,1:T(4,128)S(1)} %copy-done.3, f32[64,32,64]{2,0,1:T(8,128)S(1)} %fusion.24, f32[64,32,64]{2,1,0:T(8,128)S(1)} %get-tuple-element.8), kind=kOutput, calls=%fused_computation.21 | convolution fusion | flops 101638144 | bytes 2686976 | tf_op jit(solution)/shard_map/bks,st->bkt/dot_general | solution.py:25
  47.5 1.7 %fusion.18 = f32[64,32,64]{2,1,0:T(8,128)S(1)} fusion(f32[64,32,64]{2,0,1:T(8,128)S(1)} %get-tuple-element.5), kind=kOutput, calls=%fused_computation.36 | convolution fusion | flops 100720640 | bytes 1048576 | tf_op jit(solution)/shard_map/bks,st->bkt/dot_general | solution.py:25
  49.2 1.9 %fusion.14 = f32[64,32,64]{2,1,0:T(8,128)S(1)} fusion(f32[64,32,64]{2,0,1:T(8,128)S(1)} %get-tuple-element.6), kind=kOutput, calls=%fused_computation.32 | convolution fusion | flops 100720640 | bytes 1048576 | tf_op jit(solution)/shard_map/bks,st->bkt/dot_general | solution.py:25
  51.1 1.8 %convolution_subtract_fusion = f32[64,32,64]{2,1,0:T(8,128)S(1)} fusion(f32[64,32,64]{2,1,0:T(8,128)S(1)} %fusion.18, f32[64,32,64]{2,0,1:T(8,128)S(1)} %get-tuple-element.6), kind=kOutput, calls=%fused_computation.7 | convolution fusion | flops 100851712 | bytes 1572864 | tf_op jit(solution)/shard_map/bks,st->bkt/dot_general | solution.py:25
  52.9 1.7 %convolution_add_fusion = f32[64,32,64]{2,1,0:T(8,128)S(1)} fusion(f32[64,32,64]{2,1,0:T(8,128)S(1)} %fusion.14, f32[64,32,64]{2,0,1:T(8,128)S(1)} %get-tuple-element.5), kind=kOutput, calls=%fused_computation.6 | convolution fusion | flops 100851712 | bytes 1572864 | tf_op jit(solution)/shard_map/bks,st->bkt/dot_general | solution.py:25
  54.6 0.8 fusion.10
  55.5 1.5 %fusion.3 = f32[64,16,64]{2,1,0:T(8,128)S(1)} fusion(f32[64,64,16]{1,2,0:T(8,128)S(1)} %fusion.10, f32[64,32,64]{2,1,0:T(8,128)S(1)} %convolution_subtract_fusion, f32[64,32,64]{2,1,0:T(8,128)S(1)} %convolution_add_fusion, f32[32,64]{1,0:T(8,128)S(1)} %get-tuple-element.12, f32[32,64]{1,0:T(8,128)} %copy-done.2, f32[32,32]{0,1:T(8,128)S(1)} %copy-done.5), kind=kOutput, calls=%fused_computation.15 | convolution fusion | flops 25690112 | bytes 1593344 | tf_op jit(solution)/shard_map/kn,bns->bks/dot_general | solution.py:21
  57.0 0.8 reshape.80
  57.8 1.1 %fusion.35 = bf16[64,8,128]{2,0,1:T(8,128)(2,1)S(1)} fusion(f32[64,8,128]{2,1,0:T(8,128)} %reshape.80, f32[64]{0:T(128)} %dynamic_slice.7, bf16[8,64,128]{2,1,0:T(8,128)(2,1)S(1)} %all-to-all-done), kind=kLoop, calls=%fused_computation.60 | loop fusion | flops 262144 | bytes 524544 | tf_op jit(solution)/shard_map/convert_element_type | solution.py:128
  58.9 9.7 %all_to_all.23 = bf16[64,8,128]{2,0,1:T(8,128)(2,1)S(1)} all-to-all(bf16[64,8,128]{2,0,1:T(8,128)(2,1)S(1)} %fusion.35), channel_id=1, replica_groups=mesh['ctx'=8,'tp'=4] {'ctx'}, dimensions={1} | all-to-all | bytes 262144 | tf_op jit(solution)/shard_map/all_to_all | solution.py:129
  68.7 1.3 %fusion = bf16[2048,128]{0,1:T(8,128)(2,1)} fusion(bf16[512,128]{1,0:T(8,128)(2,1)S(1)} %fusion.34, bf16[512,2048]{1,0:T(8,128)(2,1)S(1)} %copy-done), kind=kOutput, calls=%fused_computation.1 | convolution fusion | flops 268697600 | bytes 2752512 | tf_op jit(solution)/shard_map/dot_general | solution.py:132
  70.0 19.6 %reduce-scatter.2.cloned.1.call-done = bf16[512,128]{0,1:T(8,128)(2,1)} async-done(((bf16[2048,128]{0,1:T(8,128)(2,1)}), bf16[512,128]{0,1:T(8,128)(2,1)}) %reduce-scatter.2.cloned.1.call-update) | async-done | bytes 131088 | tf_op jit(solution)/shard_map/reduce_scatter | solution.py:131
  89.5 1.7 %copy.35 = bf16[512,128]{1,0:T(8,128)(2,1)} copy(bf16[512,128]{0,1:T(8,128)(2,1)} %reduce-scatter.2.cloned.1.call-done) | data formatting | bytes 262144 | tf_op jit(solution)/shard_map/reduce_scatter | solution.py:131
  (28 shorter events, 1.7 us)
Async XLA Ops:
  6.5 62.1 %copy-start = (bf16[512,2048]{1,0:T(8,128)(2,1)S(1)}, bf16[512,2048]{1,0:T(8,128)(2,1)}, u32[]{:S(2)}) copy-start(bf16[512,2048]{1,0:T(8,128)(2,1)} %param.9) | copy-start | bytes 6291460
  6.5 15.6 %copy-start.1 = (bf16[3,512,128]{2,1,0:T(8,128)(2,1)S(1)}, bf16[3,512,128]{2,1,0:T(8,128)(2,1)}, u32[]{:S(2)}) copy-start(bf16[3,512,128]{2,1,0:T(8,128)(2,1)} %param.5) | copy-start | bytes 1179652
  6.5 9.6 %copy-start.6 = (f32[3,3,512]{2,1,0:T(4,128)S(1)}, f32[3,3,512]{2,1,0:T(4,128)}, u32[]{:S(2)}) copy-start(f32[3,3,512]{2,1,0:T(4,128)} %param.6) | copy-start | bytes 55300
  8.6 13.5 %collective-permute-start = (bf16[3,512,2]{2,1,0:T(8,128)(2,1)}, bf16[3,512,2]{2,1,0:T(8,128)(2,1)S(1)}, u32[]{:S(2)}, u32[]{:S(2)}) collective-permute-start(bf16[3,512,2]{2,1,0:T(8,128)(2,1)} %slice.49), channel_id=1, source_target_pairs={{0,4},{4,8},{8,12},{12,16},{16,20},{20,24},{24,28},{1,5},{5,9},{9,... | collective-permute-start | bytes 18440 | tf_op jit(solution)/shard_map/ppermute | solution.py:17
  13.7 25.6 %copy-start.4 = (f32[32,32]{0,1:T(8,128)}, f32[32,32]{0,1:T(8,128)S(1)}, u32[]{:S(2)}) copy-start(f32[32,32]{0,1:T(8,128)S(1)} %fusion.84) | copy-start | bytes 12292
  13.8 40.8 %copy-start.2 = (f32[32,64]{1,0:T(8,128)}, f32[32,64]{1,0:T(8,128)S(1)}, u32[]{:S(2)}) copy-start(f32[32,64]{1,0:T(8,128)S(1)} %get-tuple-element.13) | copy-start | bytes 24580
  24.4 14.0 %all-to-all-start = ((bf16[8,64,128]{2,1,0:T(8,128)(2,1)}), bf16[8,64,128]{2,1,0:T(8,128)(2,1)S(1)}, u32[]{:S(2)}, u32[]{:S(2)}) async-start(bf16[8,64,128]{2,1,0:T(8,128)(2,1)} %bitcast.4), calls=%async_computation | async-start | bytes 262144 | tf_op jit(solution)/shard_map/all_to_all | solution.py:112
  31.1 58.5 %reduce-scatter.2.cloned.1.call-start = ((), (), s32[]{:S(2)}) async-start(), calls=%async_computation.3 | async-start | bytes 655360 | tf_op jit(solution)/shard_map/reduce_scatter | solution.py:131
  43.7 1.8 %copy-start.3 = (f32[4,32,64]{2,0,1:T(4,128)S(1)}, f32[4,32,64]{2,0,1:T(4,128)}, u32[]{:S(2)}) copy-start(f32[4,32,64]{2,0,1:T(4,128)} %copy.24) | copy-start | bytes 98308
  54.6 0.8 copy-start.5
Sparse Core Ops, SparseCore 0:
  70.1 19.3 reduce-scatter.1
where the time goes:
time: 98.6 us; the launch traced here: 98 us
  waiting for transfers between devices  30.3 us (31%)
  matrix products  21.3 us (22%)
  between operations  13.7 us (14%)
  starting transfers between devices  11.8 us (12%)
  blocking collectives  9.74 us (10%)
  local copies, waits for them, and re-layouts  7.7 us (8%)
  other arithmetic  3.54 us (4%)
    reduce_scatter x1, waiting for transfers between devices, local(): lax.psum_scatter(lax.dot_general(out_weight, gated, (((0,), (0,)), ((), (...  19.6 us
    dot_general x12, matrix products, right_product(): return jnp.einsum('bks,st->bkt', stacked, matrix, precision=highest)  15.8 us
    all_to_all x1, blocking collectives, local(): lax.all_to_all(long_mix, 'ctx', split_axis=1, concat_axis=0, tiled=True)  9.74 us
    all_to_all x1, starting transfers between devices, local(): lax.all_to_all(product, 'ctx', split_axis=0, concat_axis=1, tiled=True)  6.69 us
    ppermute x1, waiting for transfers between devices, from_behind(): lax.ppermute(value, axis, [(source, source + steps) for source in range(i...  5.9 us
    ppermute x1, starting transfers between devices, from_behind(): lax.ppermute(value, axis, [(source, source + steps) for source in range(i...  4.88 us
    all_to_all x1, waiting for transfers between devices, local(): lax.all_to_all(product, 'ctx', split_axis=0, concat_axis=1, tiled=True)  4.81 us
    dot_general x6, matrix products, left_product(): return jnp.einsum('kn,bns->bks', matrix, stacked, precision=highest)  4.19 us
  transfers between devices with their start and end apart: 3, of which 3 were waited for; matrix products, arithmetic and copies ran while one was open for 5% of the time, Pallas kernels for 0%

commit v1 on v0

--- a/solution.py
+++ b/solution.py
@@ -1,8 +1,11 @@
+import functools
 import math
 
 import jax
 import jax.numpy as jnp
 from jax import lax
+from jax.experimental import pallas as pl
+from jax.experimental.pallas import tpu as pltpu
 from jax.sharding import PartitionSpec as P
 
 GROUP = 16
@@ -138,8 +141,326 @@
     )
 
 
+LANES = 128
+NT = (((1,), (1,)), ((), ()))
+NN = (((1,), (0,)), ((), ()))
+
+
+def block_kernel(
+    ctx_count, pieces, halves,
+    features, short_taps, filters, skip_gain, weight_hbm, out,
+    weight, weight_turned, taps_rows, taps, filters_wide, toeplitz,
+    halo_tx, halo_rx, kv, kv_rx, mix_tx, mix_rx, query, gated,
+    sib_tx, sib_rx, far_tx, far_rx,
+    weight_sem, halo_send, halo_recv, kv_send, kv_recv, mix_send, mix_recv,
+    sib_send, sib_recv, far_send, far_recv,
+):
+    taps_count = short_taps.shape[0]
+    chan_tp, tok = features.shape[1:]
+    chan_dev = chan_tp // ctx_count
+    group_dev = chan_dev // GROUP
+    out_dev = out.shape[0]
+    me = lax.axis_index("ctx")
+    rank = lax.axis_index("tp")
+    core = lax.rem(rank, 2)
+    sibling = rank + 1 - 2 * core
+    far = lax.rem(rank + 2, 4)
+
+    load_weight = pltpu.make_async_copy(weight_hbm, weight, weight_sem)
+    load_weight.start()
+
+    barrier = pltpu.get_barrier_semaphore()
+    for step in range(1, ctx_count):
+        pl.semaphore_signal(
+            barrier, inc=1, device_id={"ctx": lax.rem(me + step, ctx_count)},
+            device_id_type=pl.DeviceIdType.MESH,
+        )
+    for other in (sibling, far):
+        pl.semaphore_signal(
+            barrier, inc=1, device_id={"tp": other}, device_id_type=pl.DeviceIdType.MESH
+        )
+
+    halo_rows = halo_tx.shape[0]
+    row_of = lax.broadcasted_iota(jnp.int32, (halo_rows, tok), 0)
+    col_of = lax.broadcasted_iota(jnp.int32, (halo_rows, tok), 1)
+    edge = jnp.zeros((halo_rows, chan_tp), jnp.float32)
+    for row in range(3):
+        pick = (row_of - row * (taps_count - 1) == col_of - (tok - taps_count + 1)) & (
+            row_of >= row * (taps_count - 1)
+        ) & (row_of < (row + 1) * (taps_count - 1))
+        edge += lax.dot_general(
+            pick.astype(jnp.bfloat16), features[row], NT, preferred_element_type=jnp.float32
+        )
+    halo_tx[...] = edge.astype(jnp.bfloat16)
+
+    pl.semaphore_wait(barrier, ctx_count + 1)
+
+    def halo_copy():
+        return pltpu.make_async_remote_copy(
+            src_ref=halo_tx, dst_ref=halo_rx, send_sem=halo_send, recv_sem=halo_recv,
+            device_id={"ctx": lax.rem(me + 1, ctx_count)},
+            device_id_type=pl.DeviceIdType.MESH,
+        )
+
+    @pl.when(me < ctx_count - 1)
+    def _():
+        halo_copy().start()
+
+    taps_rows[...] = jnp.zeros_like(taps_rows)
+    for offset in range(taps_count):
+        taps_rows[3 * offset : 3 * offset + 3, :] = short_taps[offset]
+    taps_rows[3 * taps_count : 3 * taps_count + 1, :] = skip_gain[...]
+    taps[...] = taps_rows[...].T
+
+    @pl.when(me > 0)
+    def _():
+        halo_copy().wait_recv()
+
+    @pl.when(me == 0)
+    def _():
+        halo_rx[...] = jnp.zeros_like(halo_rx)
+
+    halo = halo_rx[...].astype(jnp.float32).T
+    lane = lax.broadcasted_iota(jnp.int32, (chan_tp, tok), 1)
+
+    def short_conv(row):
+        values = features[row].astype(jnp.float32)
+        total = taps[:, row : row + 1] * values
+        for offset in range(1, taps_count):
+            moved = pltpu.roll(values, offset, 1)
+            for place in range(offset):
+                column = row * (taps_count - 1) + taps_count - 1 - offset + place
+                moved = jnp.where(lane == place, halo[:, column : column + 1], moved)
+            index = 3 * offset + row
+            total = total + taps[:, index : index + 1] * moved
+        return total
+
+    kv[...] = (short_conv(1) * short_conv(2)).astype(jnp.bfloat16)
+
+    part = chan_dev // pieces
+
+    def kv_copy(step, piece):
+        target = lax.rem(me + step, ctx_count)
+        begin = pl.multiple_of(target * chan_dev + piece * part, part)
+        return pltpu.make_async_remote_copy(
+            src_ref=kv.at[pl.ds(begin, part)],
+            dst_ref=kv_rx.at[me, pl.ds(piece * part, part)],
+            send_sem=kv_send.at[piece, step], recv_sem=kv_recv.at[piece, step],
+            device_id={"ctx": target}, device_id_type=pl.DeviceIdType.MESH,
+        )
+
+    def mix_copy(step, piece):
+        target = lax.rem(me + step, ctx_count)
+        begin = pl.multiple_of(me * chan_dev + piece * part, part)
+        return pltpu.make_async_remote_copy(
+            src_ref=mix_tx.at[target, pl.ds(piece * part, part)],
+            dst_ref=mix_rx.at[pl.ds(begin, part)],
+            send_sem=mix_send.at[piece, step], recv_sem=mix_recv.at[piece, step],
+            device_id={"ctx": target}, device_id_type=pl.DeviceIdType.MESH,
+        )
+
+    order = sorted(range(1, ctx_count), key=lambda step: -min(step, ctx_count - step))
+    for piece in range(pieces):
+        for step in order:
+            kv_copy(step, piece).start()
+    own = pl.ds(pl.multiple_of(me * chan_dev, chan_dev), chan_dev)
+    kv_rx[me] = kv[own, :]
+
+    filters_wide[...] = filters[...].astype(jnp.float32)
+    length = filters.shape[1]
+    wide_row = lax.broadcasted_iota(jnp.int32, (tok, length), 0)
+    wide_col = lax.broadcasted_iota(jnp.int32, (tok, length), 1)
+    for group in range(group_dev):
+        taps_long = filters_wide[pl.ds(me * group_dev + group, 1), :]
+        spread = pltpu.roll(
+            jnp.broadcast_to(taps_long, (tok, length)), 0, 1, stride=1, stride_axis=0
+        )
+        toeplitz[group] = jnp.where(wide_col >= wide_row, spread, 0.0).astype(jnp.bfloat16)
+    query[...] = short_conv(0)
+    load_weight.wait()
+    turn = 256
+
+    @pl.loop(0, weight.shape[1] // turn)
+    def _(index):
+        begin = pl.multiple_of(index * turn, turn)
+        weight_turned[pl.ds(begin, turn), :] = weight[:, pl.ds(begin, turn)].T
+
+    groups_part = group_dev // pieces
+    for piece in range(pieces):
+        for step in order:
+            kv_copy(step, piece).wait_recv()
+        for group in range(piece * groups_part, (piece + 1) * groups_part):
+            rows = slice(group * GROUP, (group + 1) * GROUP)
+            signal = kv_rx[:, rows, :].reshape(ctx_count * GROUP, tok)
+            begin = pl.multiple_of(me * chan_dev + group * GROUP, GROUP)
+            column = 3 * taps_count
+            direct = taps[pl.ds(begin, GROUP), :][:, column : column + 1]
+            totals = [
+                direct * kv_rx[block, rows, :].astype(jnp.float32) for block in range(ctx_count)
+            ]
+            wide = 2 if ctx_count % 2 == 0 else 1
+            for distance in range(0, ctx_count, wide):
+                products = lax.dot_general(
+                    signal[: (ctx_count - distance) * GROUP],
+                    toeplitz[group, :, distance * tok : (distance + wide) * tok],
+                    NN, preferred_element_type=jnp.float32,
+                )
+                for more in range(wide):
+                    for block in range(distance + more, ctx_count):
+                        source = block - distance - more
+                        totals[block] += products[
+                            source * GROUP : (source + 1) * GROUP, more * tok : (more + 1) * tok
+                        ]
+            for block in range(ctx_count):
+                mix_tx[block, rows, :] = totals[block].astype(jnp.bfloat16)
+        for step in order:
+            mix_copy(step, piece).start()
+    mix_rx[own, :] = mix_tx[me]
+
+    for piece in range(pieces):
+        for step in order:
+            mix_copy(step, piece).wait_recv()
+    gated[...] = (query[...] * mix_rx[...].astype(jnp.float32)).astype(jnp.bfloat16)
+
+    rows_half = out_dev // halves
+
+    def partial(owner, half):
+        begin = pl.multiple_of(owner * out_dev + half * rows_half, rows_half)
+        return lax.dot_general(
+            weight_turned[pl.ds(begin, rows_half), :], gated[...], NN,
+            preferred_element_type=jnp.float32,
+        )
+
+    def half_of(half):
+        return pl.ds(half * rows_half, rows_half)
+
+    def sib_copy(slot, half):
+        return pltpu.make_async_remote_copy(
+            src_ref=sib_tx.at[slot, half_of(half)], dst_ref=sib_rx.at[slot, half_of(half)],
+            send_sem=sib_send.at[slot, half], recv_sem=sib_recv.at[slot, half],
+            device_id={"tp": sibling}, device_id_type=pl.DeviceIdType.MESH,
+        )
+
+    def far_copy(half):
+        return pltpu.make_async_remote_copy(
+            src_ref=far_tx.at[half_of(half)], dst_ref=far_rx.at[half_of(half)],
+            send_sem=far_send.at[half], recv_sem=far_recv.at[half],
+            device_id={"tp": far}, device_id_type=pl.DeviceIdType.MESH,
+        )
+
+    far_sibling = lax.rem(sibling + 2, 4)
+    for half in range(halves):
+        sib_tx[0, half_of(half), :] = partial(far_sibling, half).astype(jnp.bfloat16)
+        sib_copy(0, half).start()
+    for half in range(halves):
+        mine = partial(far, half)
+        sib_copy(0, half).wait_recv()
+        far_tx[half_of(half), :] = (
+            mine + sib_rx[0, half_of(half), :].astype(jnp.float32)
+        ).astype(jnp.bfloat16)
+        far_copy(half).start()
+    for half in range(halves):
+        sib_tx[1, half_of(half), :] = partial(sibling, half).astype(jnp.bfloat16)
+        sib_copy(1, half).start()
+    for half in range(halves):
+        mine = partial(rank, half)
+        sib_copy(1, half).wait_recv()
+        mine += sib_rx[1, half_of(half), :].astype(jnp.float32)
+        far_copy(half).wait_recv()
+        out[half_of(half), :] = (
+            mine + far_rx[half_of(half), :].astype(jnp.float32)
+        ).astype(jnp.bfloat16)
+
+    @pl.when(me < ctx_count - 1)
+    def _():
+        halo_copy().wait_send()
+
+    for piece in range(pieces):
+        for step in order:
+            kv_copy(step, piece).wait_send()
+            mix_copy(step, piece).wait_send()
+    for half in range(halves):
+        sib_copy(0, half).wait_send()
+        sib_copy(1, half).wait_send()
+        far_copy(half).wait_send()
+
+
+def fused(features, short_taps, filters, skip_gain, out_weight):
+    taps_count = short_taps.shape[0]
+    _, chan_tp, tok = features.shape
+    ctx_count = lax.axis_size("ctx")
+    group_rows, length = filters.shape
+    chan_dev = chan_tp // ctx_count
+    group_dev = chan_dev // GROUP
+    out_all = out_weight.shape[1]
+    out_dev = out_all // lax.axis_size("tp")
+    pieces = 2 if group_dev % 2 == 0 else 1
+    halves = 2
+    bf16, f32 = jnp.bfloat16, jnp.float32
+    vmem = pl.BlockSpec(memory_space=pltpu.VMEM)
+    dma = pltpu.SemaphoreType.DMA
+    return pl.pallas_call(
+        functools.partial(block_kernel, ctx_count, pieces, halves),
+        out_shape=jax.ShapeDtypeStruct((out_dev, tok), bf16),
+        in_specs=[vmem] * 4 + [pl.BlockSpec(memory_space=pl.ANY)],
+        out_specs=vmem,
+        scratch_shapes=[
+            pltpu.VMEM((chan_tp, out_all), bf16),
+            pltpu.VMEM((out_all, chan_tp), bf16),
+            pltpu.VMEM((16, chan_tp), f32),
+            pltpu.VMEM((chan_tp, 16), f32),
+            pltpu.VMEM((group_rows, length), f32),
+            pltpu.VMEM((group_dev, tok, length), bf16),
+            pltpu.VMEM((16, chan_tp), bf16),
+            pltpu.VMEM((16, chan_tp), bf16),
+            pltpu.VMEM((chan_tp, tok), bf16),
+            pltpu.VMEM((ctx_count, chan_dev, tok), bf16),
+            pltpu.VMEM((ctx_count, chan_dev, tok), bf16),
+            pltpu.VMEM((chan_tp, tok), bf16),
+            pltpu.VMEM((chan_tp, tok), f32),
+            pltpu.VMEM((chan_tp, tok), bf16),
+            pltpu.VMEM((2, out_dev, tok), bf16),
+            pltpu.VMEM((2, out_dev, tok), bf16),
+            pltpu.VMEM((out_dev, tok), bf16),
+            pltpu.VMEM((out_dev, tok), bf16),
+            dma, dma, dma,
+            dma((pieces, ctx_count)), dma((pieces, ctx_count)),
+            dma((pieces, ctx_count)), dma((pieces, ctx_count)),
+            dma((2, halves)), dma((2, halves)),
+            dma((halves,)), dma((halves,)),
+        ],
+        compiler_params=pltpu.CompilerParams(
+            collective_id=0, has_side_effects=True, vmem_limit_bytes=40 * 2**20
+        ),
+    )(features, short_taps, filters, skip_gain.reshape(1, chan_tp), out_weight)
+
+
+def fits_kernel(mesh, features, short_taps, filters, skip_gain, out_weight):
+    ctx_count, tp_count = mesh.shape["ctx"], mesh.shape["tp"]
+    rows, channels, tokens = features.shape
+    taps_count = short_taps.shape[0]
+    tok = tokens // ctx_count
+    chan_tp = channels // tp_count
+    toeplitz_bytes = chan_tp // ctx_count // GROUP * tok * tokens * 2
+    return (
+        tp_count == 4
+        and tok == LANES
+        and rows * (taps_count - 1) <= 16
+        and rows * taps_count < 16
+        and chan_tp % (ctx_count * GROUP) == 0
+        and chan_tp % LANES == 0
+        and out_weight.shape[1] % (tp_count * 256) == 0
+        and toeplitz_bytes <= 2**22
+    )
+
+
 def solution(mesh):
     placed = (P(None, "tp", "ctx"), P(None, None, "tp"), P("tp", None), P("tp"), P("tp", None))
-    return jax.shard_map(
-        local, mesh=mesh, in_specs=placed, out_specs=P("tp", "ctx"), check_vma=False
-    )
+
+    def run(*arrays):
+        body = fused if fits_kernel(mesh, *arrays) else local
+        return jax.shard_map(
+            body, mesh=mesh, in_specs=placed, out_specs=P("tp", "ctx"), check_vma=False
+        )(*arrays)
+
+    return run

time: 98.6 us -> 31.9 us (0.32)
  waiting for transfers between devices: 30.3 us -> 0 us
  Pallas kernels: 0 us -> 26.1 us
  matrix products: 21.3 us -> 0 us
  between operations: 13.7 us -> 0.01 us
  starting transfers between devices: 11.8 us -> 0 us
  blocking collectives: 9.74 us -> 0 us
  other arithmetic: 3.54 us -> 0 us
  local copies, waits for them, and re-layouts: 7.7 us -> 5.5 us
    pallas_call x0 -> x1, Pallas kernels: none -> 26.1 us  [fused(): pl.pallas_call(functools.partial(block_kernel, ctx_count, pieces, halves)...]
    dot_general x19 -> x0, matrix products: 21.3 us -> none  [the longest x12 15.8 us: right_product(): return jnp.einsum('bks,st->bkt', stacked, matrix, precision=highest)]
    reduce_scatter x1 -> x0, waiting for transfers between devices: 19.6 us -> none  [local(): lax.psum_scatter(lax.dot_general(out_weight, gated, (((0,), (0,)), ((), (...]
    all_to_all x1 -> x0, blocking collectives: 9.74 us -> none  [local(): lax.all_to_all(long_mix, 'ctx', split_axis=1, concat_axis=0, tiled=True)]
    all_to_all x1 -> x0, starting transfers between devices: 6.69 us -> none  [local(): lax.all_to_all(product, 'ctx', split_axis=0, concat_axis=1, tiled=True)]
    ppermute x1 -> x0, waiting for transfers between devices: 5.9 us -> none  [from_behind(): lax.ppermute(value, axis, [(source, source + steps) for source in range(i...]
    unnamed x14 -> x11, local copies, waits for them, and re-layouts: 0.03 us -> 5.5 us
    ppermute x1 -> x0, starting transfers between devices: 4.88 us -> none  [from_behind(): lax.ppermute(value, axis, [(source, source + steps) for source in range(i...]
  transfers between devices with their start and end apart: 3 -> 0, of which waited for: 3 -> 0; matrix products, arithmetic and copies ran while one was open for 5% -> 0% of each run, Pallas kernels for 0% -> 0%
where the time goes in v1:
time: 31.9 us; the launch traced here: 31.6 us
  Pallas kernels  26.1 us (82%)
  local copies, waits for them, and re-layouts  5.5 us (17%)
    pallas_call x1, Pallas kernels, fused(): pl.pallas_call(functools.partial(block_kernel, ctx_count, pieces, halves)...  26.1 us
    unnamed x11, local copies, waits for them, and re-layouts  5.5 us

profile of v1, /device:TPU:0, one launch (start us, length us, event | category | flops | bytes accessed | tf_op | source)
XLA Modules:
  0.0 31.6 jit_solution(6180996930958804790)
XLA Ops:
  0.0 0.0 copy-start
  0.0 1.6 %copy-done = bf16[512,2048]{1,0:T(8,128)(2,1)S(1)} copy-done((bf16[512,2048]{1,0:T(8,128)(2,1)S(1)}, bf16[512,2048]{1,0:T(8,128)(2,1)}, u32[]{:S(2)}) %copy-start) | copy-done | bytes 2097176
  1.6 0.0 copy-start.1
  1.6 1.0 %copy-done.1 = bf16[3,512,128]{2,1,0:T(8,128)(2,1)S(1)} copy-done((bf16[3,512,128]{2,1,0:T(8,128)(2,1)S(1)}, bf16[3,512,128]{2,1,0:T(8,128)(2,1)}, u32[]{:S(2)}) %copy-start.1) | copy-done | bytes 393240
  2.6 0.0 copy-start.2
  2.6 0.8 %copy-done.2 = bf16[32,1024]{1,0:T(8,128)(2,1)S(1)} copy-done((bf16[32,1024]{1,0:T(8,128)(2,1)S(1)}, bf16[32,1024]{1,0:T(8,128)(2,1)}, u32[]{:S(2)}) %copy-start.2) | copy-done | bytes 65560
  3.4 0.0 copy-start.3
  3.4 0.7 %copy-done.3 = f32[3,3,512]{2,1,0:T(4,128)S(1)} copy-done((f32[3,3,512]{2,1,0:T(4,128)S(1)}, f32[3,3,512]{2,1,0:T(4,128)}, u32[]{:S(2)}) %copy-start.3) | copy-done | bytes 18456
  4.2 0.0 copy-start.4
  4.2 0.7 %copy-done.4 = f32[512]{0:T(512)S(1)} copy-done((f32[512]{0:T(512)S(1)}, f32[512]{0:T(512)}, u32[]{:S(2)}) %copy-start.4) | copy-done | bytes 2072
  4.8 26.1 %shard_map.55 = bf16[512,128]{1,0:T(8,128)(2,1)S(1)} custom-call(bf16[3,512,128]{2,1,0:T(8,128)(2,1)S(1)} %copy-done.1, f32[3,3,512]{2,1,0:T(4,128)S(1)} %copy-done.3, bf16[32,1024]{1,0:T(8,128)(2,1)S(1)} %copy-done.2, f32[1,512]{1,0:T(1,128)S(1)} %bitcast.1, bf16[512,2048]{1,0:T(8,128)(2,1)S(1)} %copy-done), custom_call_target="tpu_custom_call" | custom-call | tf_op jit(solution)/shard_map/pallas_call | solution.py:402
  31.0 0.7 %copy.7 = bf16[512,128]{1,0:T(8,128)(2,1)} copy(bf16[512,128]{1,0:T(8,128)(2,1)S(1)} %shard_map.55) | data formatting | bytes 262144
Async XLA Ops:
  0.0 1.6 %copy-start = (bf16[512,2048]{1,0:T(8,128)(2,1)S(1)}, bf16[512,2048]{1,0:T(8,128)(2,1)}, u32[]{:S(2)}) copy-start(bf16[512,2048]{1,0:T(8,128)(2,1)} %weight_hbm.1) | copy-start | bytes 6291460
  1.6 1.0 %copy-start.1 = (bf16[3,512,128]{2,1,0:T(8,128)(2,1)S(1)}, bf16[3,512,128]{2,1,0:T(8,128)(2,1)}, u32[]{:S(2)}) copy-start(bf16[3,512,128]{2,1,0:T(8,128)(2,1)} %features.1) | copy-start | bytes 1179652
  2.6 0.8 %copy-start.2 = (bf16[32,1024]{1,0:T(8,128)(2,1)S(1)}, bf16[32,1024]{1,0:T(8,128)(2,1)}, u32[]{:S(2)}) copy-start(bf16[32,1024]{1,0:T(8,128)(2,1)} %filters.1) | copy-start | bytes 196612
  3.4 0.7 %copy-start.3 = (f32[3,3,512]{2,1,0:T(4,128)S(1)}, f32[3,3,512]{2,1,0:T(4,128)}, u32[]{:S(2)}) copy-start(f32[3,3,512]{2,1,0:T(4,128)} %short_taps.1) | copy-start | bytes 55300
  4.2 0.7 %copy-start.4 = (f32[512]{0:T(512)S(1)}, f32[512]{0:T(512)}, u32[]{:S(2)}) copy-start(f32[512]{0:T(512)} %param.8) | copy-start | bytes 6148

commit v2 on v1

--- a/solution.py
+++ b/solution.py
@@ -148,13 +148,22 @@
 
 def block_kernel(
     ctx_count, pieces, halves,
-    features, short_taps, filters, skip_gain, weight_hbm, out,
-    weight, weight_turned, taps_rows, taps, filters_wide, toeplitz,
+    features_hbm, short_taps_hbm, filters_hbm, skip_gain_hbm, weight_hbm, out,
+    features, short_taps, filters, skip_gain, weight, weight_turned, taps_rows, taps, filters_wide, toeplitz,
     halo_tx, halo_rx, kv, kv_rx, mix_tx, mix_rx, query, gated,
     sib_tx, sib_rx, far_tx, far_rx,
-    weight_sem, halo_send, halo_recv, kv_send, kv_recv, mix_send, mix_recv,
+    load_sem, halo_send, halo_recv, kv_send, kv_recv, mix_send, mix_recv,
     sib_send, sib_recv, far_send, far_recv,
 ):
+    loads = [
+        pltpu.make_async_copy(source, target, load_sem.at[index])
+        for index, (source, target) in enumerate((
+            (features_hbm, features), (short_taps_hbm, short_taps), (skip_gain_hbm, skip_gain),
+            (filters_hbm, filters), (weight_hbm, weight),
+        ))
+    ]
+    for load in loads:
+        load.start()
     taps_count = short_taps.shape[0]
     chan_tp, tok = features.shape[1:]
     chan_dev = chan_tp // ctx_count
@@ -166,9 +175,6 @@
     sibling = rank + 1 - 2 * core
     far = lax.rem(rank + 2, 4)
 
-    load_weight = pltpu.make_async_copy(weight_hbm, weight, weight_sem)
-    load_weight.start()
-
     barrier = pltpu.get_barrier_semaphore()
     for step in range(1, ctx_count):
         pl.semaphore_signal(
@@ -183,6 +189,7 @@
     halo_rows = halo_tx.shape[0]
     row_of = lax.broadcasted_iota(jnp.int32, (halo_rows, tok), 0)
     col_of = lax.broadcasted_iota(jnp.int32, (halo_rows, tok), 1)
+    loads[0].wait()
     edge = jnp.zeros((halo_rows, chan_tp), jnp.float32)
     for row in range(3):
         pick = (row_of - row * (taps_count - 1) == col_of - (tok - taps_count + 1)) & (
@@ -207,6 +214,8 @@
         halo_copy().start()
 
     taps_rows[...] = jnp.zeros_like(taps_rows)
+    loads[1].wait()
+    loads[2].wait()
     for offset in range(taps_count):
         taps_rows[3 * offset : 3 * offset + 3, :] = short_taps[offset]
     taps_rows[3 * taps_count : 3 * taps_count + 1, :] = skip_gain[...]
@@ -266,6 +275,7 @@
     own = pl.ds(pl.multiple_of(me * chan_dev, chan_dev), chan_dev)
     kv_rx[me] = kv[own, :]
 
+    loads[3].wait()
     filters_wide[...] = filters[...].astype(jnp.float32)
     length = filters.shape[1]
     wide_row = lax.broadcasted_iota(jnp.int32, (tok, length), 0)
@@ -277,14 +287,6 @@
         )
         toeplitz[group] = jnp.where(wide_col >= wide_row, spread, 0.0).astype(jnp.bfloat16)
     query[...] = short_conv(0)
-    load_weight.wait()
-    turn = 256
-
-    @pl.loop(0, weight.shape[1] // turn)
-    def _(index):
-        begin = pl.multiple_of(index * turn, turn)
-        weight_turned[pl.ds(begin, turn), :] = weight[:, pl.ds(begin, turn)].T
-
     groups_part = group_dev // pieces
     for piece in range(pieces):
         for step in order:
@@ -316,6 +318,13 @@
         for step in order:
             mix_copy(step, piece).start()
     mix_rx[own, :] = mix_tx[me]
+    loads[4].wait()
+    turn = 256
+
+    @pl.loop(0, weight.shape[1] // turn)
+    def _(index):
+        begin = pl.multiple_of(index * turn, turn)
+        weight_turned[pl.ds(begin, turn), :] = weight[:, pl.ds(begin, turn)].T
 
     for piece in range(pieces):
         for step in order:
@@ -397,14 +406,17 @@
     pieces = 2 if group_dev % 2 == 0 else 1
     halves = 2
     bf16, f32 = jnp.bfloat16, jnp.float32
-    vmem = pl.BlockSpec(memory_space=pltpu.VMEM)
     dma = pltpu.SemaphoreType.DMA
     return pl.pallas_call(
         functools.partial(block_kernel, ctx_count, pieces, halves),
         out_shape=jax.ShapeDtypeStruct((out_dev, tok), bf16),
-        in_specs=[vmem] * 4 + [pl.BlockSpec(memory_space=pl.ANY)],
-        out_specs=vmem,
+        in_specs=[pl.BlockSpec(memory_space=pltpu.HBM)] * 5,
+        out_specs=pl.BlockSpec(memory_space=pltpu.VMEM),
         scratch_shapes=[
+            pltpu.VMEM(features.shape, bf16),
+            pltpu.VMEM(short_taps.shape, f32),
+            pltpu.VMEM(filters.shape, bf16),
+            pltpu.VMEM((1, chan_tp), f32),
             pltpu.VMEM((chan_tp, out_all), bf16),
             pltpu.VMEM((out_all, chan_tp), bf16),
             pltpu.VMEM((16, chan_tp), f32),
@@ -423,14 +435,14 @@
             pltpu.VMEM((2, out_dev, tok), bf16),
             pltpu.VMEM((out_dev, tok), bf16),
             pltpu.VMEM((out_dev, tok), bf16),
-            dma, dma, dma,
+            dma((5,)), dma, dma,
             dma((pieces, ctx_count)), dma((pieces, ctx_count)),
             dma((pieces, ctx_count)), dma((pieces, ctx_count)),
             dma((2, halves)), dma((2, halves)),
             dma((halves,)), dma((halves,)),
         ],
         compiler_params=pltpu.CompilerParams(
-            collective_id=0, has_side_effects=True, vmem_limit_bytes=40 * 2**20
+            collective_id=0, has_side_effects=True, vmem_limit_bytes=62 * 2**20
         ),
     )(features, short_taps, filters, skip_gain.reshape(1, chan_tp), out_weight)
 

time: 31.9 us -> 28.5 us (0.89)
  local copies, waits for them, and re-layouts: 5.5 us -> 1.57 us
  Pallas kernels: 26.1 us -> 26.7 us
    unnamed x11 -> x1, local copies, waits for them, and re-layouts: 5.5 us -> 1.57 us
    pallas_call x1, Pallas kernels: 26.1 us -> 26.7 us  [fused(): pl.pallas_call(functools.partial(block_kernel, ctx_count, pieces, halves)...]
where the time goes in v2:
time: 28.5 us; the launch traced here: 28.3 us
  Pallas kernels  26.7 us (94%)
  local copies, waits for them, and re-layouts  1.57 us (6%)
    pallas_call x1, Pallas kernels, fused(): pl.pallas_call(functools.partial(block_kernel, ctx_count, pieces, halves)...  26.7 us
    unnamed x1, local copies, waits for them, and re-layouts  1.57 us

profile of v2, /device:TPU:0, one launch (start us, length us, event | category | flops | bytes accessed | tf_op | source)
XLA Modules:
  0.0 28.3 jit_solution(952990194432484247)
XLA Ops:
  0.0 26.7 %shard_map.55 = bf16[512,128]{1,0:T(8,128)(2,1)} custom-call(bf16[3,512,128]{2,1,0:T(8,128)(2,1)} %features_hbm.1, f32[3,3,512]{2,1,0:T(4,128)} %short_taps_hbm.1, bf16[32,1024]{1,0:T(8,128)(2,1)} %filters_hbm.1, f32[1,512]{1,0:T(1,128)} %bitcast.1, bf16[512,2048]{1,0:T(8,128)(2,1)} %weight_hbm.1), custom_call_target="tpu_custom_call" | custom-call | tf_op jit(solution)/shard_map/pallas_call | solution.py:410
  26.7 1.6 %copy.7 = bf16[512,128]{1,0:T(8,128)(2,1)} copy(bf16[512,128]{1,0:T(8,128)(2,1)} %shard_map.55) | data formatting | bytes 262144

commit v3 on v2

--- a/solution.py
+++ b/solution.py
@@ -150,9 +150,9 @@
     ctx_count, pieces, halves,
     features_hbm, short_taps_hbm, filters_hbm, skip_gain_hbm, weight_hbm, out,
     features, short_taps, filters, skip_gain, weight, weight_turned, taps_rows, taps, filters_wide, toeplitz,
-    halo_tx, halo_rx, kv, kv_rx, mix_tx, mix_rx, query, gated,
+    halo_tx, halo_rx, edge_rx, edge_columns, kv, kv_rx, mix_tx, mix_rx, query, gated,
     sib_tx, sib_rx, far_tx, far_rx,
-    load_sem, halo_send, halo_recv, kv_send, kv_recv, mix_send, mix_recv,
+    load_sem, halo_send, halo_recv, edge_send, edge_recv, kv_send, kv_recv, mix_send, mix_recv,
     sib_send, sib_recv, far_send, far_recv,
 ):
     loads = [
@@ -186,33 +186,6 @@
             barrier, inc=1, device_id={"tp": other}, device_id_type=pl.DeviceIdType.MESH
         )
 
-    halo_rows = halo_tx.shape[0]
-    row_of = lax.broadcasted_iota(jnp.int32, (halo_rows, tok), 0)
-    col_of = lax.broadcasted_iota(jnp.int32, (halo_rows, tok), 1)
-    loads[0].wait()
-    edge = jnp.zeros((halo_rows, chan_tp), jnp.float32)
-    for row in range(3):
-        pick = (row_of - row * (taps_count - 1) == col_of - (tok - taps_count + 1)) & (
-            row_of >= row * (taps_count - 1)
-        ) & (row_of < (row + 1) * (taps_count - 1))
-        edge += lax.dot_general(
-            pick.astype(jnp.bfloat16), features[row], NT, preferred_element_type=jnp.float32
-        )
-    halo_tx[...] = edge.astype(jnp.bfloat16)
-
-    pl.semaphore_wait(barrier, ctx_count + 1)
-
-    def halo_copy():
-        return pltpu.make_async_remote_copy(
-            src_ref=halo_tx, dst_ref=halo_rx, send_sem=halo_send, recv_sem=halo_recv,
-            device_id={"ctx": lax.rem(me + 1, ctx_count)},
-            device_id_type=pl.DeviceIdType.MESH,
-        )
-
-    @pl.when(me < ctx_count - 1)
-    def _():
-        halo_copy().start()
-
     taps_rows[...] = jnp.zeros_like(taps_rows)
     loads[1].wait()
     loads[2].wait()
@@ -221,30 +194,57 @@
     taps_rows[3 * taps_count : 3 * taps_count + 1, :] = skip_gain[...]
     taps[...] = taps_rows[...].T
 
-    @pl.when(me > 0)
-    def _():
-        halo_copy().wait_recv()
-
-    @pl.when(me == 0)
-    def _():
-        halo_rx[...] = jnp.zeros_like(halo_rx)
-
-    halo = halo_rx[...].astype(jnp.float32).T
+    edges = taps_count - 1
+    slots = halo_tx.shape[0]
+    slot_of = lax.broadcasted_iota(jnp.int32, (slots, tok), 0)
+    col_of = lax.broadcasted_iota(jnp.int32, (slots, tok), 1)
+    loads[0].wait()
+    edge = jnp.zeros((slots, chan_tp), jnp.float32)
+    for row, first_slot, count in ((1, 0, 2 * edges), (2, 2 * edges, 2 * edges), (0, 4 * edges, edges)):
+        inner = slot_of - first_slot
+        wanted = jnp.where(inner < edges, tok - edges + inner, inner - edges)
+        pick = (inner >= 0) & (inner < count) & (col_of == wanted)
+        edge += lax.dot_general(
+            pick.astype(jnp.bfloat16), features[row], NT, preferred_element_type=jnp.float32
+        )
+    halo_tx[...] = edge.astype(jnp.bfloat16)
+
     lane = lax.broadcasted_iota(jnp.int32, (chan_tp, tok), 1)
 
-    def short_conv(row):
+    def short_conv(row, halo):
         values = features[row].astype(jnp.float32)
         total = taps[:, row : row + 1] * values
         for offset in range(1, taps_count):
             moved = pltpu.roll(values, offset, 1)
-            for place in range(offset):
-                column = row * (taps_count - 1) + taps_count - 1 - offset + place
-                moved = jnp.where(lane == place, halo[:, column : column + 1], moved)
+            if halo is not None:
+                for place in range(offset):
+                    column = 4 * edges + edges - offset + place
+                    moved = jnp.where(lane == place, halo[:, column : column + 1], moved)
             index = 3 * offset + row
             total = total + taps[:, index : index + 1] * moved
         return total
 
-    kv[...] = (short_conv(1) * short_conv(2)).astype(jnp.bfloat16)
+    kv[...] = (short_conv(1, None) * short_conv(2, None)).astype(jnp.bfloat16)
+
+    pl.semaphore_wait(barrier, ctx_count + 1)
+
+    def halo_copy():
+        return pltpu.make_async_remote_copy(
+            src_ref=halo_tx, dst_ref=halo_rx, send_sem=halo_send, recv_sem=halo_recv,
+            device_id={"ctx": lax.rem(me + 1, ctx_count)},
+            device_id_type=pl.DeviceIdType.MESH,
+        )
+
+    def tile_of(target):
+        return pl.ds(pl.multiple_of(target * chan_dev // LANES * LANES, LANES), LANES)
+
+    def edge_copy(step):
+        target = lax.rem(me + step, ctx_count)
+        return pltpu.make_async_remote_copy(
+            src_ref=halo_tx.at[:, tile_of(target)], dst_ref=edge_rx.at[me],
+            send_sem=edge_send.at[step], recv_sem=edge_recv.at[step],
+            device_id={"ctx": target}, device_id_type=pl.DeviceIdType.MESH,
+        )
 
     part = chan_dev // pieces
 
@@ -272,8 +272,17 @@
     for piece in range(pieces):
         for step in order:
             kv_copy(step, piece).start()
+        if piece == 0:
+            for step in order:
+                edge_copy(step).start()
+
+    @pl.when(me < ctx_count - 1)
+    def _():
+        halo_copy().start()
+
     own = pl.ds(pl.multiple_of(me * chan_dev, chan_dev), chan_dev)
     kv_rx[me] = kv[own, :]
+    edge_rx[me] = halo_tx[:, tile_of(me)]
 
     loads[3].wait()
     filters_wide[...] = filters[...].astype(jnp.float32)
@@ -286,19 +295,59 @@
             jnp.broadcast_to(taps_long, (tok, length)), 0, 1, stride=1, stride_axis=0
         )
         toeplitz[group] = jnp.where(wide_col >= wide_row, spread, 0.0).astype(jnp.bfloat16)
-    query[...] = short_conv(0)
+
+    @pl.when(me > 0)
+    def _():
+        halo_copy().wait_recv()
+
+    @pl.when(me == 0)
+    def _():
+        halo_rx[...] = jnp.zeros_like(halo_rx)
+
+    query[...] = short_conv(0, halo_rx[...].astype(jnp.float32).T)
+
+    for step in order:
+        edge_copy(step).wait_recv()
+    spots = ctx_count * slots
+    edge_columns[...] = edge_rx[...].astype(jnp.float32).reshape(spots, LANES).T
+    begin = pl.multiple_of(me * chan_dev % LANES, GROUP)
+    here = edge_columns[pl.ds(begin, chan_dev), :]
+    spot = lax.broadcasted_iota(jnp.int32, (chan_dev, spots), 1)
+    slot = spot % slots
+    before = jnp.where(spot < slots, 0.0, pltpu.roll(here, slots, 1))
+    series = jnp.where(slot % (2 * edges) < edges, before, here)
+    own_taps = taps[own, :]
+    edge_conv = jnp.zeros((chan_dev, spots), jnp.float32)
+    for offset in range(taps_count):
+        index = 3 * offset
+        factor = jnp.where(
+            slot < 2 * edges, own_taps[:, index + 1 : index + 2], own_taps[:, index + 2 : index + 3]
+        )
+        moved = series if offset == 0 else pltpu.roll(series, offset, 1)
+        edge_conv = edge_conv + factor * moved
+    mended = edge_conv * pltpu.roll(edge_conv, spots - 2 * edges, 1)
+    place_of = lax.broadcasted_iota(jnp.int32, (GROUP, tok), 1)
     groups_part = group_dev // pieces
     for piece in range(pieces):
         for step in order:
             kv_copy(step, piece).wait_recv()
         for group in range(piece * groups_part, (piece + 1) * groups_part):
             rows = slice(group * GROUP, (group + 1) * GROUP)
-            signal = kv_rx[:, rows, :].reshape(ctx_count * GROUP, tok)
+            blocks = []
+            for block in range(ctx_count):
+                values = kv_rx[block, rows, :].astype(jnp.float32)
+                for place in range(edges):
+                    column = block * slots + edges + place
+                    values = jnp.where(
+                        place_of == place, mended[rows, column : column + 1], values
+                    )
+                blocks.append(values.astype(jnp.bfloat16))
+            signal = jnp.concatenate(blocks, axis=0)
             begin = pl.multiple_of(me * chan_dev + group * GROUP, GROUP)
             column = 3 * taps_count
             direct = taps[pl.ds(begin, GROUP), :][:, column : column + 1]
             totals = [
-                direct * kv_rx[block, rows, :].astype(jnp.float32) for block in range(ctx_count)
+                direct * blocks[block].astype(jnp.float32) for block in range(ctx_count)
             ]
             wide = 2 if ctx_count % 2 == 0 else 1
             for distance in range(0, ctx_count, wide):
@@ -384,6 +433,8 @@
     def _():
         halo_copy().wait_send()
 
+    for step in order:
+        edge_copy(step).wait_send()
     for piece in range(pieces):
         for step in order:
             kv_copy(step, piece).wait_send()
@@ -425,6 +476,8 @@
             pltpu.VMEM((group_dev, tok, length), bf16),
             pltpu.VMEM((16, chan_tp), bf16),
             pltpu.VMEM((16, chan_tp), bf16),
+            pltpu.VMEM((ctx_count, 16, LANES), bf16),
+            pltpu.VMEM((LANES, ctx_count * 16), f32),
             pltpu.VMEM((chan_tp, tok), bf16),
             pltpu.VMEM((ctx_count, chan_dev, tok), bf16),
             pltpu.VMEM((ctx_count, chan_dev, tok), bf16),
@@ -436,15 +489,19 @@
             pltpu.VMEM((out_dev, tok), bf16),
             pltpu.VMEM((out_dev, tok), bf16),
             dma((5,)), dma, dma,
+            dma((ctx_count,)), dma((ctx_count,)),
             dma((pieces, ctx_count)), dma((pieces, ctx_count)),
             dma((pieces, ctx_count)), dma((pieces, ctx_count)),
             dma((2, halves)), dma((2, halves)),
             dma((halves,)), dma((halves,)),
         ],
         compiler_params=pltpu.CompilerParams(
-            collective_id=0, has_side_effects=True, vmem_limit_bytes=62 * 2**20
+            collective_id=0, has_side_effects=True, vmem_limit_bytes=40 * 2**20
         ),
-    )(features, short_taps, filters, skip_gain.reshape(1, chan_tp), out_weight)
+    )(*(
+        pltpu.with_memory_space_constraint(value, pltpu.HBM)
+        for value in (features, short_taps, filters, skip_gain.reshape(1, chan_tp), out_weight)
+    ))
 
 
 def fits_kernel(mesh, features, short_taps, filters, skip_gain, out_weight):
@@ -457,7 +514,9 @@
     return (
         tp_count == 4
         and tok == LANES
-        and rows * (taps_count - 1) <= 16
+        and 5 * (taps_count - 1) <= 16
+        and ctx_count * 16 % LANES == 0
+        and LANES % (chan_tp // ctx_count) == 0
         and rows * taps_count < 16
         and chan_tp % (ctx_count * GROUP) == 0
         and chan_tp % LANES == 0

time: 28.5 us -> 24.5 us (0.86)
  Pallas kernels: 26.7 us -> 23.7 us
  local copies, waits for them, and re-layouts: 1.57 us -> 0.66 us
    pallas_call x1, Pallas kernels: 26.7 us -> 23.7 us  [fused(): pl.pallas_call(functools.partial(block_kernel, ctx_count, pieces, halves)...]
    unnamed x1, local copies, waits for them, and re-layouts: 1.57 us -> 0.66 us
where the time goes in v3:
time: 24.5 us; the launch traced here: 24.3 us
  Pallas kernels  23.7 us (97%)
  local copies, waits for them, and re-layouts  0.66 us (3%)
    pallas_call x1, Pallas kernels, fused(): pl.pallas_call(functools.partial(block_kernel, ctx_count, pieces, halves)...  23.7 us
    unnamed x1, local copies, waits for them, and re-layouts  0.66 us

profile of v3, /device:TPU:0, one launch (start us, length us, event | category | flops | bytes accessed | tf_op | source)
XLA Modules:
  0.0 24.3 jit_solution(13174554006495772197)
XLA Ops:
  0.0 23.7 %shard_map.55 = bf16[512,128]{1,0:T(8,128)(2,1)S(1)} custom-call(bf16[3,512,128]{2,1,0:T(8,128)(2,1)} %features_hbm.1, f32[3,3,512]{2,1,0:T(4,128)} %short_taps_hbm.1, bf16[32,1024]{1,0:T(8,128)(2,1)} %filters_hbm.1, f32[1,512]{1,0:T(1,128)} %bitcast.1, bf16[512,2048]{1,0:T(8,128)(2,1)} %weight_hbm.1), custom_call_target="tpu_custom_call" | custom-call | tf_op jit(solution)/shard_map/pallas_call | solution.py:461
  23.7 0.7 %copy.7 = bf16[512,128]{1,0:T(8,128)(2,1)} copy(bf16[512,128]{1,0:T(8,128)(2,1)S(1)} %shard_map.55) | data formatting | bytes 262144

commit v4 on v3

--- a/solution.py
+++ b/solution.py
@@ -162,8 +162,7 @@
             (filters_hbm, filters), (weight_hbm, weight),
         ))
     ]
-    for load in loads:
-        load.start()
+    loads[0].start()
     taps_count = short_taps.shape[0]
     chan_tp, tok = features.shape[1:]
     chan_dev = chan_tp // ctx_count
@@ -186,6 +185,9 @@
             barrier, inc=1, device_id={"tp": other}, device_id_type=pl.DeviceIdType.MESH
         )
 
+    for load in loads[1:]:
+        load.start()
+
     taps_rows[...] = jnp.zeros_like(taps_rows)
     loads[1].wait()
     loads[2].wait()
@@ -196,19 +198,6 @@
 
     edges = taps_count - 1
     slots = halo_tx.shape[0]
-    slot_of = lax.broadcasted_iota(jnp.int32, (slots, tok), 0)
-    col_of = lax.broadcasted_iota(jnp.int32, (slots, tok), 1)
-    loads[0].wait()
-    edge = jnp.zeros((slots, chan_tp), jnp.float32)
-    for row, first_slot, count in ((1, 0, 2 * edges), (2, 2 * edges, 2 * edges), (0, 4 * edges, edges)):
-        inner = slot_of - first_slot
-        wanted = jnp.where(inner < edges, tok - edges + inner, inner - edges)
-        pick = (inner >= 0) & (inner < count) & (col_of == wanted)
-        edge += lax.dot_general(
-            pick.astype(jnp.bfloat16), features[row], NT, preferred_element_type=jnp.float32
-        )
-    halo_tx[...] = edge.astype(jnp.bfloat16)
-
     lane = lax.broadcasted_iota(jnp.int32, (chan_tp, tok), 1)
 
     def short_conv(row, halo):
@@ -224,6 +213,8 @@
             total = total + taps[:, index : index + 1] * moved
         return total
 
+    loads[0].wait()
+
     kv[...] = (short_conv(1, None) * short_conv(2, None)).astype(jnp.bfloat16)
 
     pl.semaphore_wait(barrier, ctx_count + 1)
@@ -273,6 +264,17 @@
         for step in order:
             kv_copy(step, piece).start()
         if piece == 0:
+            slot_of = lax.broadcasted_iota(jnp.int32, (slots, tok), 0)
+            col_of = lax.broadcasted_iota(jnp.int32, (slots, tok), 1)
+            edge = jnp.zeros((slots, chan_tp), jnp.float32)
+            for row, first_slot, count in ((1, 0, 2 * edges), (2, 2 * edges, 2 * edges), (0, 4 * edges, edges)):
+                inner = slot_of - first_slot
+                wanted = jnp.where(inner < edges, tok - edges + inner, inner - edges)
+                pick = (inner >= 0) & (inner < count) & (col_of == wanted)
+                edge += lax.dot_general(
+                    pick.astype(jnp.bfloat16), features[row], NT, preferred_element_type=jnp.float32
+                )
+            halo_tx[...] = edge.astype(jnp.bfloat16)
             for step in order:
                 edge_copy(step).start()
 

time: 24.5 us -> 24.5 us (level)
  no operation moved by 1% of the time
where the time goes in v4:
time: 24.5 us; the launch traced here: 24.4 us
  Pallas kernels  23.7 us (97%)
  local copies, waits for them, and re-layouts  0.66 us (3%)
    pallas_call x1, Pallas kernels, fused(): pl.pallas_call(functools.partial(block_kernel, ctx_count, pieces, halves)...  23.7 us
    unnamed x1, local copies, waits for them, and re-layouts  0.66 us

profile of v4, /device:TPU:0, one launch (start us, length us, event | category | flops | bytes accessed | tf_op | source)
XLA Modules:
  0.0 24.4 jit_solution(8112100920989603092)
XLA Ops:
  0.0 23.7 %shard_map.55 = bf16[512,128]{1,0:T(8,128)(2,1)S(1)} custom-call(bf16[3,512,128]{2,1,0:T(8,128)(2,1)} %features_hbm.1, f32[3,3,512]{2,1,0:T(4,128)} %short_taps_hbm.1, bf16[32,1024]{1,0:T(8,128)(2,1)} %filters_hbm.1, f32[1,512]{1,0:T(1,128)} %bitcast.1, bf16[512,2048]{1,0:T(8,128)(2,1)} %weight_hbm.1), custom_call_target="tpu_custom_call" | custom-call | tf_op jit(solution)/shard_map/pallas_call | solution.py:463
  23.7 0.7 %copy.7 = bf16[512,128]{1,0:T(8,128)(2,1)} copy(bf16[512,128]{1,0:T(8,128)(2,1)S(1)} %shard_map.55) | data formatting | bytes 262144
